TPU v7x, 128 devices: a whole 4x4x4 slice. The times are simulated.
128 devices in a mesh: dom: 32 (over x, z, core), grp: 4 (over y).
Axes of the slice: x: 4, y: 4, z: 4, core: 2. Of those that a mesh axis runs over, the one named last changes fastest.
Arguments:
- x_current: bfloat16 [524288, 128], P(('dom', 'grp')), may hold values from -6 to 6
- x_cached: bfloat16 [524288, 128], P(('dom', 'grp')), may hold values from -6 to 6
- w_self: bfloat16 [128, 512], replicated, may hold values from -0.5 to 0.5
- w_neigh: bfloat16 [128, 512], replicated, may hold values from -1 to 1
- bias: float32 [512], replicated, may hold values from -3 to 3
- tile_columns: int32 [4096, 40], P(('dom', 'grp')), may hold values from 0 to 255
- tile_count: int32 [4096], P(('dom', 'grp')), may hold values from 1 to 40, as said below
- adjacency: int32 [4096, 40, 2048], P(('dom', 'grp')), may hold values from 0 to 255, as said below
- degree: int32 [524288], P(('dom', 'grp')), may hold values from 1 to 5128, as said below
- boundary_blocks: int32 [128, 1], P(('dom', 'grp')), may hold values from 0 to 31
Outputs:
- hidden: bfloat16 [524288, 512], P(('dom', 'grp'))
Inputs may be any that keep to these rules, and one draw needn't show every extreme that they name: `tile_count`: every device has a row block with all 40 slots live. `adjacency`: 8 entries of a tile row packed into each word, bit b for column 8 c + b. `degree`: at least the number of ones in the row of the live tiles of the node's row block.
All inputs are finite; a program needn't handle non-finite values.
Results may differ from a plain program's by a relative error of at most 0.0025.
Values may be sent and summed in bfloat16 or wider, within the bound.
A program may use at most 192 MiB of HBM per device.

v0:
```python
import math

import jax
import jax.numpy as jnp
from jax import lax
from jax.sharding import PartitionSpec as P


def on_device(
    x_current,
    x_cached,
    w_self,
    w_neigh,
    bias,
    tile_columns,
    tile_count,
    adjacency,
    degree,
    boundary_blocks,
):
    node_rows, width = x_current.shape
    row_blocks, per_tile = tile_columns.shape
    tile_rows = node_rows // row_blocks
    chosen = x_cached.reshape(row_blocks, tile_rows, width)[boundary_blocks[0]]
    received = lax.all_gather(x_current, "grp", axis=0, tiled=True)
    part_blocks = received.reshape(-1, tile_rows, width)
    partial_value = lax.all_gather(chosen[None, None], "grp", axis=1, tiled=True)
    halo_blocks = lax.all_gather(partial_value, "dom", axis=0, tiled=True)
    block_table = jnp.concatenate([part_blocks, halo_blocks.reshape(-1, tile_rows, width)], axis=0)
    group_size = math.gcd(4, row_blocks)
    turns = row_blocks // group_size
    shifts = jnp.arange(8, dtype=jnp.int32)

    def one_group(pieces):
        columns, counts, packed = pieces
        bit_values = (
            packed.reshape(group_size, per_tile, tile_rows, tile_rows // 8, 1) >> shifts & 1
        )
        live_mask = (jnp.arange(per_tile, dtype=jnp.int32)[None, :] < counts[:, None]).astype(
            jnp.int32
        )
        adjacent = (
            bit_values.reshape(group_size, per_tile, tile_rows, tile_rows)
            * live_mask[:, :, None, None]
        ).astype(jnp.bfloat16)
        gathered = block_table[columns]
        return jnp.einsum("stij,stjf->sif", adjacent, gathered, preferred_element_type=jnp.float32)

    totals = lax.map(
        one_group,
        (
            tile_columns.reshape(turns, group_size, per_tile),
            tile_count.reshape(turns, group_size),
            adjacency.reshape(turns, group_size, per_tile, -1),
        ),
    )
    totals = totals.reshape(node_rows, width)
    average = (totals / degree.astype(jnp.float32)[:, None]).astype(jnp.bfloat16)
    summed = (
        jnp.dot(x_current, w_self, preferred_element_type=jnp.float32)
        + jnp.dot(average, w_neigh, preferred_element_type=jnp.float32)
        + bias
    )
    return jnp.maximum(summed, 0.0).astype(jnp.bfloat16)


def solution(mesh):
    in_specs = (
        P(("dom", "grp"), None),
        P(("dom", "grp"), None),
        P(),
        P(),
        P(),
        P(("dom", "grp"), None),
        P(("dom", "grp")),
        P(("dom", "grp"), None, None),
        P(("dom", "grp")),
        P(("dom", "grp"), None),
    )
    out_specs = P(("dom", "grp"), None)
    return jax.shard_map(
        on_device, mesh=mesh, in_specs=in_specs, out_specs=out_specs, check_vma=False
    )
```

profile of v0, /device:TPU:0, one launch (start us, length us, event | category | flops | bytes accessed | tf_op | source)
XLA Modules:
  0.0 341.9 jit_solution(17156375614477139263)
XLA Ops:
  8.0 13.3 %all-gather = bf16[4,128,128]{2,1,0:T(8,128)(2,1)} all-gather(bf16[1,128,128]{2,1,0:T(8,128)(2,1)S(1)} %constant_dynamic-slice_fusion.2), channel_id=2, replica_groups=mesh['dom'=32,'grp'=4] {'grp'}, dimensions={0}, use_global_device_ids=true | all-gather | bytes 163840 | tf_op jit(solution)/shard_map/all_gather | solution.py:27
  21.4 20.6 %copy.16 = s32[32,40,2048]{1,2,0:T(8,128)} copy(s32[32,40,2048]{2,1,0:T(8,128)} %param.19) | data formatting | bytes 20971520 | tf_op args[7]
  42.1 4.4 %fusion.21 = f32[4096,512]{1,0:T(8,128)} fusion(bf16[4096,128]{1,0:T(8,128)(2,1)S(1)} %copy-done.2, bf16[128,512]{1,0:T(8,128)(2,1)S(1)} %copy-done.3), kind=kOutput, calls=%fused_computation.26 | convolution fusion | flops 536870912 | bytes 9568256 | tf_op jit(solution)/shard_map/dot_general | solution.py:60
  46.5 13.3 %all-gather.5.cloned.1.call-done = bf16[16384,128]{1,0:T(8,128)(2,1)} async-done(((bf16[4096,128]{1,0:T(8,128)(2,1)}), bf16[16384,128]{1,0:T(8,128)(2,1)}) %all-gather.5.cloned.1.call-update) | async-done | bytes 4194320 | tf_op jit(solution)/shard_map/all_gather | solution.py:25
  59.8 49.0 %all-gather.7.cloned.1.call-done = bf16[128,128,128]{2,1,0:T(8,128)(2,1)} async-done(((bf16[4,128,128]{2,1,0:T(8,128)(2,1)}), bf16[128,128,128]{2,1,0:T(8,128)(2,1)}) %all-gather.7.cloned.1.call-update) | async-done | bytes 4194320 | tf_op jit(solution)/shard_map/all_gather | solution.py:28
  108.8 7.4 %pad_maximum_fusion = bf16[256,128,128]{2,1,0:T(8,128)(2,1)} fusion(bf16[128,128,128]{2,1,0:T(8,128)(2,1)} %all-gather.7.cloned.1.call-done, bf16[128,128,128]{2,1,0:T(8,128)(2,1)} %bitcast.63), kind=kLoop, calls=%fused_computation.21 | loop fusion | flops 4194304 | bytes 16777216 | tf_op jit(solution)/shard_map/concatenate | solution.py:29
  116.2 210.2 %while.12 = (s32[]{:T(128)}, f32[8,4,128,128]{3,2,1,0:T(8,128)}, s32[8,4,40,2048]{2,3,1,0:T(8,128)}, s32[8,4]{1,0:T(8,128)S(1)}, s32[8,4,40]{2,1,0:T(4,128)}, /*index=5*/bf16[256,128,128]{2,1,0:T(8,128)(2,1)}, s32[]{:T(128)}) while((s32[]{:T(128)}, f32[8,4,128,128]{3,2,1,0:T(8,128)}, s32[8,4,40,2048]{2,3,1,0:T(8,128)}, ...), condition=%wide.region_1.2_spmd.clone, body=%wide.region_0.1_spmd.clone.sunk | while | flops 681576256 | bytes 22556296 | solution.py:49
  117.0 11.2 %gather_fusion = bf16[160,128,128]{2,1,0:T(8,128)(2,1)} fusion(bf16[256,128,128]{2,1,0:T(8,128)(2,1)} %get-tuple-element.136, s32[1024]{0:T(1024)S(1)} %pad_clamp_fusion.2), kind=kCustom, calls=%fused_computation.clone.clone.1 | custom fusion | bytes 10486400 | tf_op jit(solution)/shard_map/while/body/eval_jaxpr/gather | solution.py:46
  128.2 4.5 %constant_dynamic-slice_fusion.4 = s32[1,4,40,2048]{2,3,1,0:T(8,128)} fusion(s32[8,4,40,2048]{2,3,1,0:T(8,128)} %get-tuple-element.133, s32[]{:T(128)} %get-tuple-element.124), kind=kLoop, calls=%fused_computation.18.clone.1 | loop fusion | bytes 2621444 | tf_op jit(solution)/shard_map/while/body/jit(dynamic_index_in_dim)/dynamic_slice | solution.py:49
  136.2 6.3 %fusion.36 = f32[8,4,128,128]{3,2,1,0:T(8,128)} fusion(f32[8,4,128,128]{3,2,1,0:T(8,128)} %get-tuple-element.125, s32[]{:T(128)} %get-tuple-element.124, bf16[4,40,128,128]{3,2,1,0:T(8,128)(2,1)} %bitcast.61, s32[4,40]{1,0:T(4,128)S(1)} %fusion.35, s32[128]{0:T(128)S(1)} %shift_right_arithmetic.64, s32[4,40,128,16]{2,3,1,0:T(8,128)S(1)} %copy.20), kind=kOutput, calls=%fused_computation.12.clone.1 | convolution fusion | flops 681574400 | bytes 6817408 | tf_op jit(solution)/shard_map/while/body/eval_jaxpr/stij,stjf->sif/dot_general | solution.py:47
  143.3 11.2 %gather_fusion = bf16[160,128,128]{2,1,0:T(8,128)(2,1)} fusion(bf16[256,128,128]{2,1,0:T(8,128)(2,1)} %get-tuple-element.136, s32[1024]{0:T(1024)S(1)} %pad_clamp_fusion.2), kind=kCustom, calls=%fused_computation.clone.clone.1 | custom fusion | bytes 10486400 | tf_op jit(solution)/shard_map/while/body/eval_jaxpr/gather | solution.py:46
  154.4 4.5 %constant_dynamic-slice_fusion.4 = s32[1,4,40,2048]{2,3,1,0:T(8,128)} fusion(s32[8,4,40,2048]{2,3,1,0:T(8,128)} %get-tuple-element.133, s32[]{:T(128)} %get-tuple-element.124), kind=kLoop, calls=%fused_computation.18.clone.1 | loop fusion | bytes 2621444 | tf_op jit(solution)/shard_map/while/body/jit(dynamic_index_in_dim)/dynamic_slice | solution.py:49
  162.5 6.3 %fusion.36 = f32[8,4,128,128]{3,2,1,0:T(8,128)} fusion(f32[8,4,128,128]{3,2,1,0:T(8,128)} %get-tuple-element.125, s32[]{:T(128)} %get-tuple-element.124, bf16[4,40,128,128]{3,2,1,0:T(8,128)(2,1)} %bitcast.61, s32[4,40]{1,0:T(4,128)S(1)} %fusion.35, s32[128]{0:T(128)S(1)} %shift_right_arithmetic.64, s32[4,40,128,16]{2,3,1,0:T(8,128)S(1)} %copy.20), kind=kOutput, calls=%fused_computation.12.clone.1 | convolution fusion | flops 681574400 | bytes 6817408 | tf_op jit(solution)/shard_map/while/body/eval_jaxpr/stij,stjf->sif/dot_general | solution.py:47
  169.5 11.2 %gather_fusion = bf16[160,128,128]{2,1,0:T(8,128)(2,1)} fusion(bf16[256,128,128]{2,1,0:T(8,128)(2,1)} %get-tuple-element.136, s32[1024]{0:T(1024)S(1)} %pad_clamp_fusion.2), kind=kCustom, calls=%fused_computation.clone.clone.1 | custom fusion | bytes 10486400 | tf_op jit(solution)/shard_map/while/body/eval_jaxpr/gather | solution.py:46
  180.7 4.5 %constant_dynamic-slice_fusion.4 = s32[1,4,40,2048]{2,3,1,0:T(8,128)} fusion(s32[8,4,40,2048]{2,3,1,0:T(8,128)} %get-tuple-element.133, s32[]{:T(128)} %get-tuple-element.124), kind=kLoop, calls=%fused_computation.18.clone.1 | loop fusion | bytes 2621444 | tf_op jit(solution)/shard_map/while/body/jit(dynamic_index_in_dim)/dynamic_slice | solution.py:49
  188.8 6.3 %fusion.36 = f32[8,4,128,128]{3,2,1,0:T(8,128)} fusion(f32[8,4,128,128]{3,2,1,0:T(8,128)} %get-tuple-element.125, s32[]{:T(128)} %get-tuple-element.124, bf16[4,40,128,128]{3,2,1,0:T(8,128)(2,1)} %bitcast.61, s32[4,40]{1,0:T(4,128)S(1)} %fusion.35, s32[128]{0:T(128)S(1)} %shift_right_arithmetic.64, s32[4,40,128,16]{2,3,1,0:T(8,128)S(1)} %copy.20), kind=kOutput, calls=%fused_computation.12.clone.1 | convolution fusion | flops 681574400 | bytes 6817408 | tf_op jit(solution)/shard_map/while/body/eval_jaxpr/stij,stjf->sif/dot_general | solution.py:47
  195.8 11.2 %gather_fusion = bf16[160,128,128]{2,1,0:T(8,128)(2,1)} fusion(bf16[256,128,128]{2,1,0:T(8,128)(2,1)} %get-tuple-element.136, s32[1024]{0:T(1024)S(1)} %pad_clamp_fusion.2), kind=kCustom, calls=%fused_computation.clone.clone.1 | custom fusion | bytes 10486400 | tf_op jit(solution)/shard_map/while/body/eval_jaxpr/gather | solution.py:46
  207.0 4.5 %constant_dynamic-slice_fusion.4 = s32[1,4,40,2048]{2,3,1,0:T(8,128)} fusion(s32[8,4,40,2048]{2,3,1,0:T(8,128)} %get-tuple-element.133, s32[]{:T(128)} %get-tuple-element.124), kind=kLoop, calls=%fused_computation.18.clone.1 | loop fusion | bytes 2621444 | tf_op jit(solution)/shard_map/while/body/jit(dynamic_index_in_dim)/dynamic_slice | solution.py:49
  215.0 6.3 %fusion.36 = f32[8,4,128,128]{3,2,1,0:T(8,128)} fusion(f32[8,4,128,128]{3,2,1,0:T(8,128)} %get-tuple-element.125, s32[]{:T(128)} %get-tuple-element.124, bf16[4,40,128,128]{3,2,1,0:T(8,128)(2,1)} %bitcast.61, s32[4,40]{1,0:T(4,128)S(1)} %fusion.35, s32[128]{0:T(128)S(1)} %shift_right_arithmetic.64, s32[4,40,128,16]{2,3,1,0:T(8,128)S(1)} %copy.20), kind=kOutput, calls=%fused_computation.12.clone.1 | convolution fusion | flops 681574400 | bytes 6817408 | tf_op jit(solution)/shard_map/while/body/eval_jaxpr/stij,stjf->sif/dot_general | solution.py:47
  222.1 11.2 %gather_fusion = bf16[160,128,128]{2,1,0:T(8,128)(2,1)} fusion(bf16[256,128,128]{2,1,0:T(8,128)(2,1)} %get-tuple-element.136, s32[1024]{0:T(1024)S(1)} %pad_clamp_fusion.2), kind=kCustom, calls=%fused_computation.clone.clone.1 | custom fusion | bytes 10486400 | tf_op jit(solution)/shard_map/while/body/eval_jaxpr/gather | solution.py:46
  233.2 4.5 %constant_dynamic-slice_fusion.4 = s32[1,4,40,2048]{2,3,1,0:T(8,128)} fusion(s32[8,4,40,2048]{2,3,1,0:T(8,128)} %get-tuple-element.133, s32[]{:T(128)} %get-tuple-element.124), kind=kLoop, calls=%fused_computation.18.clone.1 | loop fusion | bytes 2621444 | tf_op jit(solution)/shard_map/while/body/jit(dynamic_index_in_dim)/dynamic_slice | solution.py:49
  241.3 6.3 %fusion.36 = f32[8,4,128,128]{3,2,1,0:T(8,128)} fusion(f32[8,4,128,128]{3,2,1,0:T(8,128)} %get-tuple-element.125, s32[]{:T(128)} %get-tuple-element.124, bf16[4,40,128,128]{3,2,1,0:T(8,128)(2,1)} %bitcast.61, s32[4,40]{1,0:T(4,128)S(1)} %fusion.35, s32[128]{0:T(128)S(1)} %shift_right_arithmetic.64, s32[4,40,128,16]{2,3,1,0:T(8,128)S(1)} %copy.20), kind=kOutput, calls=%fused_computation.12.clone.1 | convolution fusion | flops 681574400 | bytes 6817408 | tf_op jit(solution)/shard_map/while/body/eval_jaxpr/stij,stjf->sif/dot_general | solution.py:47
  248.3 11.2 %gather_fusion = bf16[160,128,128]{2,1,0:T(8,128)(2,1)} fusion(bf16[256,128,128]{2,1,0:T(8,128)(2,1)} %get-tuple-element.136, s32[1024]{0:T(1024)S(1)} %pad_clamp_fusion.2), kind=kCustom, calls=%fused_computation.clone.clone.1 | custom fusion | bytes 10486400 | tf_op jit(solution)/shard_map/while/body/eval_jaxpr/gather | solution.py:46
  259.5 4.5 %constant_dynamic-slice_fusion.4 = s32[1,4,40,2048]{2,3,1,0:T(8,128)} fusion(s32[8,4,40,2048]{2,3,1,0:T(8,128)} %get-tuple-element.133, s32[]{:T(128)} %get-tuple-element.124), kind=kLoop, calls=%fused_computation.18.clone.1 | loop fusion | bytes 2621444 | tf_op jit(solution)/shard_map/while/body/jit(dynamic_index_in_dim)/dynamic_slice | solution.py:49
  267.6 6.3 %fusion.36 = f32[8,4,128,128]{3,2,1,0:T(8,128)} fusion(f32[8,4,128,128]{3,2,1,0:T(8,128)} %get-tuple-element.125, s32[]{:T(128)} %get-tuple-element.124, bf16[4,40,128,128]{3,2,1,0:T(8,128)(2,1)} %bitcast.61, s32[4,40]{1,0:T(4,128)S(1)} %fusion.35, s32[128]{0:T(128)S(1)} %shift_right_arithmetic.64, s32[4,40,128,16]{2,3,1,0:T(8,128)S(1)} %copy.20), kind=kOutput, calls=%fused_computation.12.clone.1 | convolution fusion | flops 681574400 | bytes 6817408 | tf_op jit(solution)/shard_map/while/body/eval_jaxpr/stij,stjf->sif/dot_general | solution.py:47
  274.6 11.2 %gather_fusion = bf16[160,128,128]{2,1,0:T(8,128)(2,1)} fusion(bf16[256,128,128]{2,1,0:T(8,128)(2,1)} %get-tuple-element.136, s32[1024]{0:T(1024)S(1)} %pad_clamp_fusion.2), kind=kCustom, calls=%fused_computation.clone.clone.1 | custom fusion | bytes 10486400 | tf_op jit(solution)/shard_map/while/body/eval_jaxpr/gather | solution.py:46
  285.8 4.5 %constant_dynamic-slice_fusion.4 = s32[1,4,40,2048]{2,3,1,0:T(8,128)} fusion(s32[8,4,40,2048]{2,3,1,0:T(8,128)} %get-tuple-element.133, s32[]{:T(128)} %get-tuple-element.124), kind=kLoop, calls=%fused_computation.18.clone.1 | loop fusion | bytes 2621444 | tf_op jit(solution)/shard_map/while/body/jit(dynamic_index_in_dim)/dynamic_slice | solution.py:49
  293.8 6.3 %fusion.36 = f32[8,4,128,128]{3,2,1,0:T(8,128)} fusion(f32[8,4,128,128]{3,2,1,0:T(8,128)} %get-tuple-element.125, s32[]{:T(128)} %get-tuple-element.124, bf16[4,40,128,128]{3,2,1,0:T(8,128)(2,1)} %bitcast.61, s32[4,40]{1,0:T(4,128)S(1)} %fusion.35, s32[128]{0:T(128)S(1)} %shift_right_arithmetic.64, s32[4,40,128,16]{2,3,1,0:T(8,128)S(1)} %copy.20), kind=kOutput, calls=%fused_computation.12.clone.1 | convolution fusion | flops 681574400 | bytes 6817408 | tf_op jit(solution)/shard_map/while/body/eval_jaxpr/stij,stjf->sif/dot_general | solution.py:47
  300.9 11.2 %gather_fusion = bf16[160,128,128]{2,1,0:T(8,128)(2,1)} fusion(bf16[256,128,128]{2,1,0:T(8,128)(2,1)} %get-tuple-element.136, s32[1024]{0:T(1024)S(1)} %pad_clamp_fusion.2), kind=kCustom, calls=%fused_computation.clone.clone.1 | custom fusion | bytes 10486400 | tf_op jit(solution)/shard_map/while/body/eval_jaxpr/gather | solution.py:46
  312.1 4.5 %constant_dynamic-slice_fusion.4 = s32[1,4,40,2048]{2,3,1,0:T(8,128)} fusion(s32[8,4,40,2048]{2,3,1,0:T(8,128)} %get-tuple-element.133, s32[]{:T(128)} %get-tuple-element.124), kind=kLoop, calls=%fused_computation.18.clone.1 | loop fusion | bytes 2621444 | tf_op jit(solution)/shard_map/while/body/jit(dynamic_index_in_dim)/dynamic_slice | solution.py:49
  320.1 6.3 %fusion.36 = f32[8,4,128,128]{3,2,1,0:T(8,128)} fusion(f32[8,4,128,128]{3,2,1,0:T(8,128)} %get-tuple-element.125, s32[]{:T(128)} %get-tuple-element.124, bf16[4,40,128,128]{3,2,1,0:T(8,128)(2,1)} %bitcast.61, s32[4,40]{1,0:T(4,128)S(1)} %fusion.35, s32[128]{0:T(128)S(1)} %shift_right_arithmetic.64, s32[4,40,128,16]{2,3,1,0:T(8,128)S(1)} %copy.20), kind=kOutput, calls=%fused_computation.12.clone.1 | convolution fusion | flops 681574400 | bytes 6817408 | tf_op jit(solution)/shard_map/while/body/eval_jaxpr/stij,stjf->sif/dot_general | solution.py:47
  328.4 6.6 %maximum_convert_fusion = bf16[4096,512]{1,0:T(8,128)(2,1)} fusion(f32[4096,512]{1,0:T(8,128)} %fusion.21, bf16[4096,128]{1,0:T(8,128)(2,1)S(1)} %fusion.20, bf16[128,512]{1,0:T(8,128)(2,1)S(1)} %copy-done.4, f32[512]{0:T(512)S(1)} %copy-done.6), kind=kOutput, calls=%fused_computation.22 | convolution fusion | flops 545259520 | bytes 13764608 | tf_op jit(solution)/shard_map/dot_general | solution.py:61
  (89 shorter events, 37.7 us)
Async XLA Ops:
  6.5 1.4 copy-start
  6.5 53.3 %all-gather.5.cloned.1.call-start = ((), (), s32[]{:S(2)}) async-start(), calls=%async_computation | async-start | bytes 5242880 | tf_op jit(solution)/shard_map/all_gather | solution.py:25
  7.3 101.5 %all-gather.7.cloned.1.call-start = ((), (), s32[]{:S(2)}) async-start(), calls=%async_computation.1 | async-start | bytes 4325376 | tf_op jit(solution)/shard_map/all_gather | solution.py:28
  21.4 20.6 %copy-start.7 = (s32[32]{0:T(128)S(1)}, s32[32]{0:T(128)}, u32[]{:S(2)}) copy-start(s32[32]{0:T(128)} %param.18) | copy-start | bytes 388
  21.4 20.7 %copy-start.5 = (s32[4096]{0:T(1024)S(1)}, s32[4096]{0:T(1024)}, u32[]{:S(2)}) copy-start(s32[4096]{0:T(1024)} %param.20) | copy-start | bytes 49156
  21.4 20.7 %copy-start.2 = (bf16[4096,128]{1,0:T(8,128)(2,1)S(1)}, bf16[4096,128]{1,0:T(8,128)(2,1)}, u32[]{:S(2)}) copy-start(bf16[4096,128]{1,0:T(8,128)(2,1)} %param.12) | copy-start | bytes 3145732
  21.4 20.7 %copy-start.3 = (bf16[128,512]{1,0:T(8,128)(2,1)S(1)}, bf16[128,512]{1,0:T(8,128)(2,1)}, u32[]{:S(2)}) copy-start(bf16[128,512]{1,0:T(8,128)(2,1)} %param.14) | copy-start | bytes 393220
  116.2 212.2 %copy-start.4 = (bf16[128,512]{1,0:T(8,128)(2,1)S(1)}, bf16[128,512]{1,0:T(8,128)(2,1)}, u32[]{:S(2)}) copy-start(bf16[128,512]{1,0:T(8,128)(2,1)} %param.15) | copy-start | bytes 393220
  116.2 212.2 %copy-start.6 = (f32[512]{0:T(512)S(1)}, f32[512]{0:T(512)}, u32[]{:S(2)}) copy-start(f32[512]{0:T(512)} %param.16) | copy-start | bytes 6148
  326.4 8.7 %copy-start.1 = (bf16[4096,128]{1,0:T(8,128)(2,1)S(1)}, bf16[4096,128]{1,0:T(8,128)(2,1)}, u32[]{:S(2)}) copy-start(bf16[4096,128]{1,0:T(8,128)(2,1)} %param.13) | copy-start | bytes 3145732
Sparse Core Ops, SparseCore 0:
  9.0 50.7 all-gather.4
  62.1 46.6 all-gather.6
where the time goes:
time: 345 us; the launch traced here: 342 us
  local copies, waits for them, and re-layouts  174 us (50%)
  waiting for transfers between devices  63 us (18%)
  matrix products  61.2 us (18%)
  other arithmetic  15.6 us (5%)
  between operations  14.2 us (4%)
  blocking collectives  13.3 us (4%)
    gather x8, local copies, waits for them, and re-layouts, one_group(): gathered = block_table[columns]  89.3 us
    dot_general x8, matrix products, one_group(): jnp.einsum('stij,stjf->sif', adjacent, gathered, preferred_element_type=j...  50.2 us
    all_gather x1, waiting for transfers between devices, on_device(): halo_blocks = lax.all_gather(partial_value, 'dom', axis=0, tiled=True)  49 us
    dynamic_slice x8, local copies, waits for them, and re-layouts, on_device(): lax.map(one_group, (tile_columns.reshape(turns, group_size, per_tile), ti...  35.8 us
    shift_right_arithmetic x24, local copies, waits for them, and re-layouts, one_group(): packed.reshape(group_size, per_tile, tile_rows, tile_rows // 8, 1) >> shifts  27.9 us
    unnamed x17, local copies, waits for them, and re-layouts  20.6 us
    all_gather x1, blocking collectives, on_device(): lax.all_gather(chosen[None, None], 'grp', axis=1, tiled=True)  13.3 us
    all_gather x1, waiting for transfers between devices, on_device(): received = lax.all_gather(x_current, 'grp', axis=0, tiled=True)  13.3 us
  transfers between devices with their start and end apart: 2, of which 2 were waited for; matrix products, arithmetic and copies ran while one was open for 7% of the time, Pallas kernels for 0%

commit v1 on v0

v1 whole, which is shorter than its diff:
```python
import jax
import jax.numpy as jnp
from jax import lax
from jax.experimental import pallas as pl
from jax.experimental.pallas import tpu as pltpu
from jax.sharding import PartitionSpec as P

MESH = pl.DeviceIdType.MESH
SIDE = 4
BLOCK = 128
RB = 32
SLOTS = 40
WORDS = 640
ROWS = RB * BLOCK
FAN = 16
CHUNK = 4
CHUNKS = RB // CHUNK


def gather_kernel(xcur, chosen, part, halo, local_sem, send_sem, recv_sem):
    dom = lax.axis_index("dom")
    y = lax.axis_index("grp")
    core = dom % 2
    z = (dom // 2) % SIDE
    x = dom // (2 * SIDE)

    def at(xx, zz, cc, yy):
        return ((xx * SIDE + zz) * 2 + cc, yy)

    up, down, far = (y + 1) % SIDE, (y + 3) % SIDE, (y + 2) % SIDE
    y_up, y_down, y_far = at(x, z, core, up), at(x, z, core, down), at(x, z, core, far)
    x_up, x_down = at((x + 1) % SIDE, z, core, y), at((x + 3) % SIDE, z, core, y)
    z_up, z_down = at(x, (z + 1) % SIDE, core, y), at(x, (z + 3) % SIDE, core, y)
    sibling = at(x, z, 1 - core, y)
    peers = [y_up, y_down, y_far, x_up, x_down, z_up, z_down, sibling]
    barrier = pltpu.get_barrier_semaphore()
    for peer in peers:
        pl.semaphore_signal(barrier, inc=1, device_id=peer, device_id_type=MESH)
    pl.semaphore_wait(barrier, len(peers))

    started = []

    def send(src, dst, sem, to):
        copy = pltpu.make_async_remote_copy(
            src_ref=src,
            dst_ref=dst,
            send_sem=send_sem.at[sem],
            recv_sem=recv_sem.at[sem],
            device_id=to,
            device_id_type=MESH,
        )
        copy.start()
        started.append(copy)

    def landed(dst, sem):
        pltpu.make_async_remote_copy(
            src_ref=dst,
            dst_ref=dst,
            send_sem=send_sem.at[sem],
            recv_sem=recv_sem.at[sem],
            device_id=sibling,
            device_id_type=MESH,
        ).wait_recv()

    def blocks(first, count):
        return halo.at[pl.ds(pl.multiple_of(first * BLOCK, BLOCK), count * BLOCK)]

    def rows(first, count):
        return part.at[pl.ds(pl.multiple_of(first, BLOCK), count)]

    base = core * 64

    def place(yy):
        ring = jnp.where(yy < 2, z * SIDE + x, x * SIDE + z)
        return base + (yy // 2) * 32 + ring * 2 + yy % 2

    own = blocks(place(y), 1)
    own_part = rows(y * ROWS, ROWS)
    block_copy = pltpu.make_async_copy(chosen, own, local_sem.at[0])
    block_copy.start()
    for sem, peer in enumerate((y_up, y_down, y_far)):
        send(chosen, own, sem, peer)
    send(xcur, own_part, 3, y_up)
    send(xcur, own_part, 4, y_down)
    part_copy = pltpu.make_async_copy(xcur, own_part, local_sem.at[1])
    part_copy.start()
    block_copy.wait()
    landed(blocks(place(down), 1), 0)
    landed(blocks(place(up), 1), 1)
    landed(blocks(place(far), 1), 2)

    first = [
        (lambda m: base + (z * SIDE + m) * 2, x, x_up, x_down),
        (lambda m: base + 32 + (x * SIDE + m) * 2, z, z_up, z_down),
    ]
    second = [
        (lambda m: base + m * 8, z, z_up, z_down),
        (lambda m: base + 32 + m * 8, x, x_up, x_down),
    ]
    for half, (piece, me, pos, neg) in enumerate(first):
        sem = 8 + 4 * half
        send(blocks(piece(me), 2), blocks(piece(me), 2), sem, pos)
        send(blocks(piece(me), 2), blocks(piece(me), 2), sem + 1, neg)
    for half, (piece, me, pos, neg) in enumerate(first):
        sem = 8 + 4 * half
        low, high = piece((me + 3) % SIDE), piece((me + 1) % SIDE)
        landed(blocks(low, 2), sem)
        send(blocks(low, 1), blocks(low, 1), sem + 2, pos)
        landed(blocks(high, 2), sem + 1)
        send(blocks(high + 1, 1), blocks(high + 1, 1), sem + 3, neg)
    for half, (piece, me, _, _) in enumerate(first):
        sem = 8 + 4 * half
        opposite = piece((me + 2) % SIDE)
        landed(blocks(opposite, 1), sem + 2)
        landed(blocks(opposite + 1, 1), sem + 3)
        piece2, me2, pos2, neg2 = second[half]
        mine = blocks(piece2(me2), 8)
        send(mine, mine, 16 + 4 * half, pos2)
        send(mine, mine, 17 + 4 * half, neg2)
        send(mine, mine, 24 + 5 * half, sibling)
    for half, (piece, me, pos, neg) in enumerate(second):
        sem = 16 + 4 * half
        low, high = piece((me + 3) % SIDE), piece((me + 1) % SIDE)
        landed(blocks(low, 8), sem)
        send(blocks(low, 4), blocks(low, 4), sem + 2, pos)
        send(blocks(low, 8), blocks(low, 8), 25 + 5 * half, sibling)
        landed(blocks(high, 8), sem + 1)
        send(blocks(high + 4, 4), blocks(high + 4, 4), sem + 3, neg)
        send(blocks(high, 8), blocks(high, 8), 26 + 5 * half, sibling)
    part_half = ROWS // 2
    landed(rows(down * ROWS, ROWS), 3)
    send(rows(down * ROWS, part_half), rows(down * ROWS, part_half), 5, y_up)
    landed(rows(up * ROWS, ROWS), 4)
    send(rows(up * ROWS + part_half, part_half), rows(up * ROWS + part_half, part_half), 6, y_down)
    for half, (piece, me, _, _) in enumerate(second):
        sem = 16 + 4 * half
        opposite = piece((me + 2) % SIDE)
        landed(blocks(opposite, 4), sem + 2)
        send(blocks(opposite, 4), blocks(opposite, 4), 27 + 5 * half, sibling)
        landed(blocks(opposite + 4, 4), sem + 3)
        send(blocks(opposite + 4, 4), blocks(opposite + 4, 4), 28 + 5 * half, sibling)
    other = (1 - core) * 64
    for half, (start, me) in enumerate(((other, z), (other + 32, x))):
        sem = 24 + 5 * half
        landed(blocks(start + me * 8, 8), sem)
        landed(blocks(start + (me + 3) % SIDE * 8, 8), sem + 1)
        landed(blocks(start + (me + 1) % SIDE * 8, 8), sem + 2)
        landed(blocks(start + (me + 2) % SIDE * 8, 4), sem + 3)
        landed(blocks(start + (me + 2) % SIDE * 8 + 4, 4), sem + 4)
    part_copy.wait()
    landed(rows(far * ROWS, part_half), 5)
    landed(rows(far * ROWS + part_half, part_half), 6)
    for copy in started:
        copy.wait_send()


def gather(xcur, chosen):
    hbm = pl.BlockSpec(memory_space=pl.ANY)
    return pl.pallas_call(
        gather_kernel,
        out_shape=(
            jax.ShapeDtypeStruct((SIDE * ROWS, BLOCK), jnp.bfloat16),
            jax.ShapeDtypeStruct((128 * BLOCK, BLOCK), jnp.bfloat16),
        ),
        in_specs=[hbm, hbm],
        out_specs=(hbm, hbm),
        scratch_shapes=[
            pltpu.SemaphoreType.DMA((2,)),
            pltpu.SemaphoreType.DMA((34,)),
            pltpu.SemaphoreType.DMA((34,)),
        ],
        compiler_params=pltpu.CompilerParams(collective_id=0, has_side_effects=True),
        name="gather",
    )(xcur, chosen)


def layer_kernel(
    cols, counts, words_hbm, part_hbm, halo_hbm, xown_hbm, w, bias, degree, out_hbm,
    groups, words, table, xown, totals, out, turned, word_sem, table_sem, out_sem,
):
    def word_copy(c):
        span = pl.ds(c * CHUNK * WORDS, CHUNK * WORDS)
        return pltpu.make_async_copy(words_hbm.at[span], words.at[span], word_sem.at[c])

    def out_copy(c):
        span = pl.ds(pl.multiple_of(c * CHUNK * BLOCK, BLOCK), CHUNK * BLOCK)
        return pltpu.make_async_copy(out.at[span], out_hbm.at[span], out_sem.at[c])

    part_copy = pltpu.make_async_copy(part_hbm, table.at[pl.ds(0, SIDE * ROWS)], table_sem.at[0])
    halo_copy = pltpu.make_async_copy(halo_hbm, table.at[pl.ds(SIDE * ROWS, 128 * BLOCK)], table_sem.at[1])
    own_copy = pltpu.make_async_copy(xown_hbm, xown, table_sem.at[2])
    for copy in (part_copy, halo_copy, own_copy):
        copy.start()
    for c in range(CHUNKS):
        word_copy(c).start()

    def list_groups(r, at):
        def one(q, at):
            groups[at] = r * 16 + q
            return at + 1

        return lax.fori_loop(0, (counts[r] + 3) // 4, one, at)

    total = lax.fori_loop(0, RB, list_groups, 0)
    for k in range(FAN):
        groups[total + k] = -1
    totals[...] = jnp.zeros_like(totals)
    for copy in (part_copy, halo_copy, own_copy):
        copy.wait()
    for c in range(CHUNKS):
        word_copy(c).wait()

    lane = lax.broadcasted_iota(jnp.int32, (16, BLOCK), 1)
    source = lane // 8
    bit = lane % 8
    low_bit = (1 << bit).astype(jnp.int16)
    high_bit = jnp.where(bit == 7, -32768, 1 << (bit + 8)).astype(jnp.int16)
    one = jnp.ones((16, BLOCK), jnp.bfloat16)
    zero = jnp.zeros((16, BLOCK), jnp.bfloat16)

    def product(at):
        code = groups[at]
        live = code >= 0
        code = jnp.maximum(code, 0)
        r = code // 16
        q = code % 16
        n = jnp.where(live, counts[r], 0)
        first = r * WORDS + (q // 2) * BLOCK + (q % 2) * 4
        packed, features = None, []
        for k in range(4):
            t = q * 4 + k
            keep = jnp.where(t < n, 255 << (8 * k) if k < 3 else -16777216, 0).astype(jnp.int32)
            word = (words[pl.ds(first + k, 16, stride=8), :] << (8 * k)) & keep
            packed = word if packed is None else packed | word
            features.append(table[pl.ds(pl.multiple_of(cols[r, t] * BLOCK, BLOCK), BLOCK), :])
        tiles = [[], [], [], []]
        for m in range(8):
            spread = jnp.take_along_axis(packed, source + 16 * m, axis=1, mode="promise_in_bounds")
            low = spread.astype(jnp.int16)
            high = (spread >> 16).astype(jnp.int16)
            for tile, half, mask in zip(tiles, (low, low, high, high), (low_bit, high_bit) * 2):
                tile.append(jnp.where((half & mask) != 0, one, zero))
        adjacent = jnp.concatenate([jnp.concatenate(tile, axis=0) for tile in tiles], axis=1)
        return r, jnp.dot(adjacent, jnp.concatenate(features, axis=0), preferred_element_type=jnp.float32)

    @pl.loop(0, (total + FAN - 1) // FAN)
    def _(step):
        for r, value in [product(step * FAN + k) for k in range(FAN)]:
            totals[pl.ds(pl.multiple_of(r * BLOCK, BLOCK), BLOCK), :] += value

    @pl.loop(0, CHUNKS)
    def _(c):
        for k in range(CHUNK):
            r = c * CHUNK + k
            span = pl.ds(pl.multiple_of(r * BLOCK, BLOCK), BLOCK)
            for m in range(8):
                turned[k, pl.ds(m, 16, stride=8), :] = totals[pl.ds(r * BLOCK + m * 16, 16), :]
            row = degree[r // 8, pl.ds(r % 8, 1), :].astype(jnp.float32)
            divisor = jnp.broadcast_to(row, (BLOCK, BLOCK)).T
            average = (turned[k] / divisor).astype(jnp.bfloat16)
            both = jnp.concatenate([xown[span, :], average], axis=1)
            hidden = jnp.dot(both, w[...], preferred_element_type=jnp.float32) + bias[...]
            out[span, :] = jnp.maximum(hidden, 0.0).astype(jnp.bfloat16)
        out_copy(c).start()

    for c in range(CHUNKS):
        out_copy(c).wait()


def layer(cols, counts, adjacency, part, halo, xown, w_self, w_neigh, bias, degree):
    words = adjacency.reshape(RB, 5, 8, 16, BLOCK).transpose(0, 1, 3, 2, 4).reshape(RB * WORDS, BLOCK)
    vmem = pl.BlockSpec(memory_space=pltpu.VMEM)
    smem = pl.BlockSpec(memory_space=pltpu.SMEM)
    hbm = pl.BlockSpec(memory_space=pl.ANY)
    return pl.pallas_call(
        layer_kernel,
        out_shape=jax.ShapeDtypeStruct((ROWS, 512), jnp.bfloat16),
        in_specs=[smem, smem, hbm, hbm, hbm, hbm, vmem, vmem, vmem],
        out_specs=hbm,
        scratch_shapes=[
            pltpu.SMEM((352,), jnp.int32),
            pltpu.VMEM((RB * WORDS, BLOCK), jnp.int32),
            pltpu.VMEM((256 * BLOCK, BLOCK), jnp.bfloat16),
            pltpu.VMEM((ROWS, BLOCK), jnp.bfloat16),
            pltpu.VMEM((ROWS, BLOCK), jnp.float32),
            pltpu.VMEM((ROWS, 512), jnp.bfloat16),
            pltpu.VMEM((CHUNK, BLOCK, BLOCK), jnp.float32),
            pltpu.SemaphoreType.DMA((CHUNKS,)),
            pltpu.SemaphoreType.DMA((3,)),
            pltpu.SemaphoreType.DMA((CHUNKS,)),
        ],
        compiler_params=pltpu.CompilerParams(vmem_limit_bytes=56 * 2**20),
        name="layer",
    )(
        cols, counts, words, part, halo, xown, jnp.concatenate([w_self, w_neigh], axis=0),
        bias.reshape(1, 512), degree.reshape(SIDE, 8, BLOCK),
    )


def table_index(columns):
    e = columns - 128
    y, core, z, x = e % 4, e // 4 % 2, e // 8 % 4, e // 32
    place = core * 64 + (y // 2) * 32 + jnp.where(y < 2, z * 4 + x, x * 4 + z) * 2 + y % 2
    return jnp.where(columns < 128, columns, 128 + place)


def on_device(
    x_current, x_cached, w_self, w_neigh, bias, tile_columns, tile_count, adjacency, degree, boundary_blocks
):
    chosen = lax.dynamic_slice(x_cached, (boundary_blocks[0, 0] * BLOCK, 0), (BLOCK, BLOCK))
    part, halo = gather(x_current, chosen)
    cols = table_index(tile_columns)
    return layer(cols, tile_count, adjacency, part, halo, x_current, w_self, w_neigh, bias, degree)


def solution(mesh):
    rows = P(("dom", "grp"), None)
    line = P(("dom", "grp"))
    return jax.shard_map(
        on_device,
        mesh=mesh,
        in_specs=(rows, rows, P(), P(), P(), rows, line, P(("dom", "grp"), None, None), line, rows),
        out_specs=rows,
        check_vma=False,
    )
```

time: 345 us -> 74.7 us (0.22)
  local copies, waits for them, and re-layouts: 174 us -> 0.62 us
  Pallas kernels: 0 us -> 70 us
  waiting for transfers between devices: 63 us -> 0 us
  matrix products: 61.2 us -> 0 us
  between operations: 14.2 us -> 0.76 us
  blocking collectives: 13.3 us -> 0 us
  other arithmetic: 15.6 us -> 3.09 us
    gather x9 -> x0, local copies, waits for them, and re-layouts: 89.3 us -> none  [the longest x8 89.3 us: one_group(): gathered = block_table[columns]]
    pallas_call x0 -> x2, Pallas kernels: none -> 70 us  [the longest x1 44.5 us: gather(): pl.pallas_call(gather_kernel, out_shape=(jax.ShapeDtypeStruct((SIDE * ROW...]
    all_gather x2 -> x0, waiting for transfers between devices: 62.3 us -> none  [the longest x1 49 us: on_device(): halo_blocks = lax.all_gather(partial_value, 'dom', axis=0, tiled=True)]
    dot_general x10 -> x0, matrix products: 61.2 us -> none  [the longest x8 50.2 us: one_group(): jnp.einsum('stij,stjf->sif', adjacent, gathered, preferred_element_type=j...]
    dynamic_slice x8 -> x1, local copies, waits for them, and re-layouts: 35.8 us -> 0.62 us  [on_device(): lax.dynamic_slice(x_cached, (boundary_blocks[0, 0] * BLOCK, 0), (BLOCK, B...]
    shift_right_arithmetic x24 -> x0, local copies, waits for them, and re-layouts: 27.9 us -> none  [one_group(): packed.reshape(group_size, per_tile, tile_rows, tile_rows // 8, 1) >> shifts]
    unnamed x17 -> x2, local copies, waits for them, and re-layouts: 20.6 us -> 0.01 us
    all_gather x1 -> x0, blocking collectives: 13.3 us -> none  [on_device(): lax.all_gather(chosen[None, None], 'grp', axis=1, tiled=True)]
  transfers between devices with their start and end apart: 2 -> 0, of which waited for: 2 -> 0; matrix products, arithmetic and copies ran while one was open for 7% -> 0% of each run, Pallas kernels for 0% -> 0%
where the time goes in v1:
time: 74.7 us; the launch traced here: 74.5 us
  Pallas kernels  70 us (94%)
  other arithmetic  3.09 us (4%)
  between operations  0.76 us (1%)
    pallas_call x1, Pallas kernels, gather(): pl.pallas_call(gather_kernel, out_shape=(jax.ShapeDtypeStruct((SIDE * ROW...  44.5 us
    pallas_call x1, Pallas kernels, layer(): pl.pallas_call(layer_kernel, out_shape=jax.ShapeDtypeStruct((ROWS, 512),...  25.5 us
    concatenate x1, other arithmetic, layer(): jnp.concatenate([w_self, w_neigh], axis=0)  1.71 us

profile of v1, /device:TPU:0, one launch (start us, length us, event | category | flops | bytes accessed | tf_op | source)
XLA Modules:
  0.0 74.5 jit_solution(13538307028452521695)
XLA Ops:
  0.0 0.0 copy-start
  0.7 1.4 %compare_select_fusion.cols = s32[32,40]{1,0:T(8,128)} fusion(s32[32,40]{1,0:T(8,128)} %param.15), kind=kLoop, calls=%fused_computation.1 | loop fusion | flops 122880 | bytes 10240 | tf_op jit(solution)/shard_map/jit(_where)/select_n | solution.py:304
  2.1 0.0 copy-done
  2.1 0.6 constant_dynamic-slice_fusion.chosen
  2.8 1.7 %pad_maximum_fusion.w = bf16[256,512]{1,0:T(8,128)(2,1)} fusion(bf16[128,512]{1,0:T(8,128)(2,1)} %param.13, bf16[128,512]{1,0:T(8,128)(2,1)} %param.12), kind=kLoop, calls=%fused_computation | loop fusion | flops 524288 | bytes 524288 | tf_op jit(solution)/shard_map/concatenate | solution.py:295
  4.5 44.5 %gather.1 = (bf16[16384,128]{1,0:T(8,128)(2,1)}, bf16[16384,128]{1,0:T(8,128)(2,1)}) custom-call(bf16[4096,128]{1,0:T(8,128)(2,1)} %xown_hbm.1, bf16[128,128]{1,0:T(8,128)(2,1)} %constant_dynamic-slice_fusion.chosen), custom_call_target="tpu_custom_call" | custom-call | tf_op jit(solution)/shard_map/gather/pallas_call | solution.py:159
  49.0 25.5 %layer.1 = bf16[4096,512]{1,0:T(8,128)(2,1)} custom-call(s32[32,40]{1,0:T(8,128)} %compare_select_fusion.cols, s32[32]{0:T(128)} %counts.1, s32[20480,128]{1,0:T(8,128)} %bitcast.8, bf16[16384,128]{1,0:T(8,128)(2,1)} %get-tuple-element.7.part_hbm, bf16[16384,128]{1,0:T(8,128)(2,1)} %get-tuple-element.8.halo_hbm, bf16[4096,128]{1,0:T(8,128)(2,1)} %xown_hbm.1, ...), custom_call_target="tpu_custom_call" | custom-call | tf_op jit(solution)/shard_map/layer/pallas_call | solution.py:275
Async XLA Ops:
  0.0 2.1 %copy-start = (bf16[4096,128]{1,0:T(8,128)(2,1)S(1)}, bf16[4096,128]{1,0:T(8,128)(2,1)}, u32[]{:S(2)}) copy-start(bf16[4096,128]{1,0:T(8,128)(2,1)} %param.11) | copy-start | bytes 3145732

commit v2 on v1

v2 whole, which is shorter than its diff:
```python
import jax
import jax.numpy as jnp
from jax import lax
from jax.experimental import pallas as pl
from jax.experimental.pallas import tpu as pltpu
from jax.sharding import PartitionSpec as P

MESH = pl.DeviceIdType.MESH
SIDE = 4
BLOCK = 128
RB = 32
SLOTS = 40
WORDS = 640
ROWS = RB * BLOCK
NEAR = 12
HALO = 20
REST = 64
WHO, LEFT = 126, 127
FAN = 8
CHUNK = 4
CHUNKS = RB // CHUNK


def sort_slots(cols, counts, me, wide, live):
    wide[...] = jnp.zeros_like(wide)
    wide[:, :SLOTS] = cols[...]
    for r in range(RB):
        live[pl.ds(r, 1), :] = jnp.full((1, BLOCK), counts[r], jnp.int32)
    c = wide[...]
    t = lax.broadcasted_iota(jnp.int32, (RB, BLOCK), 1)
    on = t < live[...]
    far = (((c >> 5) - me) & 3) == 2
    kind = jnp.where(on, jnp.where(c < 128, jnp.where(far, 2, 0), 1), 3)
    e = c - 128
    y, core, z, x = e & 3, (e >> 2) & 1, (e >> 3) & 3, (e >> 5) & 3
    place = core * 64 + (y >> 1) * 32 + jnp.where(y < 2, z * 4 + x, x * 4 + z) * 2 + (y & 1)
    index = jnp.where(c < 128, c, 128 + place)
    entry = t | (index << 10) | (1 << 18)
    both = (kind << 19) | entry
    table = jnp.zeros((RB, BLOCK), jnp.int32)
    nears = halos = rests = jnp.zeros((RB, BLOCK), jnp.int32)
    for s in range(SLOTS):
        one = jnp.broadcast_to(both[:, s : s + 1], (RB, BLOCK))
        kind = one >> 19
        near = (kind == 0) & (nears < NEAR)
        halo = (kind == 1) & (halos < HALO)
        rest = (kind < 3) & jnp.logical_not(near | halo)
        target = jnp.where(near, nears, jnp.where(halo, NEAR + halos, jnp.where(rest, REST + rests, -1)))
        table = jnp.where(target == t, one & ((1 << 19) - 1), table)
        nears += jnp.where(near, 1, 0)
        halos += jnp.where(halo, 1, 0)
        rests += jnp.where(rest, 1, 0)
    table = jnp.where(t == LEFT, rests, jnp.where(t == WHO, me, table))
    return table


class Unpack:
    def __init__(self):
        lane = lax.broadcasted_iota(jnp.int32, (16, BLOCK), 1)
        self.source = lane >> 3
        bit = lane & 7
        self.low_bit = (1 << bit).astype(jnp.int16)
        self.high_bit = jnp.where(bit == 7, -32768, 1 << (bit + 8)).astype(jnp.int16)

    def four(self, words, rows, keeps):
        one = jnp.ones((16, BLOCK), jnp.bfloat16)
        zero = jnp.zeros((16, BLOCK), jnp.bfloat16)
        packed = None
        for k, (row, keep) in enumerate(zip(rows, keeps)):
            mask = keep & (255 << (8 * k) if k < 3 else -16777216)
            word = (words[row] << (8 * k)) & mask
            packed = word if packed is None else packed | word
        tiles = [[], [], [], []]
        for m in range(8):
            spread = jnp.take_along_axis(packed, self.source + 16 * m, axis=1, mode="promise_in_bounds")
            low = spread.astype(jnp.int16)
            high = (spread >> 16).astype(jnp.int16)
            for tile, half, mask in zip(tiles, (low, low, high, high), (self.low_bit, self.high_bit) * 2):
                tile.append(jnp.where((half & mask) != 0, one, zero))
        return [jnp.concatenate(tile, axis=0) for tile in tiles]


def sum_tiles(unpack, plan, r, first, count, words, table, blocks):
    tiles, features = [], []
    for group in range(count // 4):
        entries = [plan[r, first + group * 4 + k] for k in range(4)]
        rows = [r * SLOTS + (e & 1023) for e in entries]
        tiles += unpack.four(words, rows, [-(e >> 18) for e in entries])
        for e in entries:
            block = (e >> 10) & (blocks - 1)
            features.append(table[block])
    return jnp.dot(
        jnp.concatenate(tiles, axis=1), jnp.concatenate(features, axis=0), preferred_element_type=jnp.float32
    )


def gather_kernel(
    cols_hbm, counts_hbm, exported, degree_hbm, xcur, cached_hbm, words_hbm,
    plan, words, table, totals, divisor,
    cols, counts, degree, wide, live, cached, raw, part, halo, local_sem, send_sem, recv_sem,
):
    dom = lax.axis_index("dom")
    y = lax.axis_index("grp")
    core = dom % 2
    z = (dom // 2) % SIDE
    x = dom // (2 * SIDE)

    def at(xx, zz, cc, yy):
        return ((xx * SIDE + zz) * 2 + cc, yy)

    up, down, far = (y + 1) % SIDE, (y + 3) % SIDE, (y + 2) % SIDE
    y_up, y_down, y_far = at(x, z, core, up), at(x, z, core, down), at(x, z, core, far)
    x_others = [at((x + k) % SIDE, z, core, y) for k in (3, 1, 2)]
    z_others = [at(x, (z + k) % SIDE, core, y) for k in (3, 1, 2)]
    sibling = at(x, z, 1 - core, y)
    cached_copy = pltpu.make_async_copy(cached_hbm, cached, local_sem.at[0])
    cached_copy.start()
    words_copy = pltpu.make_async_copy(words_hbm, raw, local_sem.at[2])
    words_copy.start()
    small_copies = [
        pltpu.make_async_copy(src, dst, local_sem.at[7 + k])
        for k, (src, dst) in enumerate(
            ((cols_hbm, cols), (counts_hbm, counts), (degree_hbm, degree))
        )
    ]
    for copy in small_copies:
        copy.start()
    peers = [y_up, y_down, y_far, *x_others, *z_others, sibling]
    barrier = pltpu.get_barrier_semaphore()
    for peer in peers:
        pl.semaphore_signal(barrier, inc=1, device_id=peer, device_id_type=MESH)
    pl.semaphore_wait(barrier, len(peers))

    started = []

    def send(src, dst, sem, to):
        copy = pltpu.make_async_remote_copy(
            src_ref=src,
            dst_ref=dst,
            send_sem=send_sem.at[sem],
            recv_sem=recv_sem.at[sem],
            device_id=to,
            device_id_type=MESH,
        )
        copy.start()
        started.append(copy)

    def landed(dst, sem):
        pltpu.make_async_remote_copy(
            src_ref=dst,
            dst_ref=dst,
            send_sem=send_sem.at[sem],
            recv_sem=recv_sem.at[sem],
            device_id=sibling,
            device_id_type=MESH,
        ).wait_recv()

    def blocks(first, count):
        return halo.at[pl.ds(first, count)]

    def rows(first, count):
        return part.at[pl.ds(first, count)]

    def far_rows(first):
        return table.at[pl.ds(first, RB // 2)]

    base = core * 64

    def place(yy):
        ring = jnp.where(yy < 2, z * SIDE + x, x * SIDE + z)
        return base + (yy // 2) * 32 + ring * 2 + yy % 2

    own = blocks(place(y), 1)
    own_part = rows(y * RB, RB)
    cached_copy.wait()
    for copy in small_copies:
        copy.wait()
    chosen = cached[exported[0, 0]]
    halo[place(y)] = chosen
    for sem, peer in enumerate((y_up, y_down, y_far)):
        send(own, own, sem, peer)
    send(xcur, own_part, 3, y_up)
    send(xcur, own_part, 4, y_down)
    part_copy = pltpu.make_async_copy(xcur, own_part, local_sem.at[1])
    part_copy.start()
    wide[...] = sort_slots(cols, counts, y, wide, live)
    plan_copy = pltpu.make_async_copy(wide, plan, local_sem.at[0])
    plan_copy.start()
    landed(blocks(place(down), 1), 0)
    landed(blocks(place(up), 1), 1)
    landed(blocks(place(far), 1), 2)

    first = [
        (lambda m: base + (z * SIDE + m) * 2, x, x_others),
        (lambda m: base + 32 + (x * SIDE + m) * 2, z, z_others),
    ]
    second = [
        (lambda m: base + m * 8, z, z_others),
        (lambda m: base + 32 + m * 8, x, x_others),
    ]
    for half, (piece, me, others) in enumerate(first):
        for k, other in enumerate(others):
            send(blocks(piece(me), 2), blocks(piece(me), 2), 8 + 4 * half + k, other)

    words_copy.wait()

    @pl.loop(0, RB)
    def _(r):
        for t in range(SLOTS):
            slot = raw[pl.ds(r * WORDS + (t // 8) * BLOCK + t % 8, 16, stride=8), :]
            words[r * SLOTS + t] = slot

    for half, (piece, me, _) in enumerate(first):
        for k, d in enumerate((1, 3, 2)):
            landed(blocks(piece((me + d) % SIDE), 2), 8 + 4 * half + k)
        piece2, me2, others2 = second[half]
        mine = blocks(piece2(me2), 8)
        for k in (2, 0, 1):
            send(mine, mine, 16 + 4 * half + k, others2[k])
        send(mine, mine, 24 + 4 * half, sibling)

    @pl.loop(0, RB)
    def _(r):
        row = degree[r // 8, pl.ds(r % 8, 1), :].astype(jnp.float32)
        divisor[pl.ds(pl.multiple_of(r * BLOCK, BLOCK), BLOCK), :] = jnp.broadcast_to(row, (BLOCK, BLOCK)).T

    def pass_on(k, d):
        for half, (piece, me, _) in enumerate(second):
            got = blocks(piece((me + d) % SIDE), 8)
            landed(got, 16 + 4 * half + k)
            send(got, got, 25 + 4 * half + k, sibling)

    pass_on(0, 1)
    pass_on(1, 3)
    part_half = RB // 2
    landed(rows(down * RB, RB), 3)
    send(rows(down * RB, part_half), far_rows(down * RB), 5, y_up)
    landed(rows(up * RB, RB), 4)
    send(rows(up * RB + part_half, part_half), far_rows(up * RB + part_half), 6, y_down)
    pass_on(2, 2)
    part_copy.wait()
    plan_copy.wait()
    unpack = Unpack()

    @pl.loop(0, RB // 4)
    def _(step):
        for k in range(4):
            r = step * 4 + k
            value = sum_tiles(unpack, plan, r, 0, NEAR, words, part, 128)
            totals[pl.ds(pl.multiple_of(r * BLOCK, BLOCK), BLOCK), :] = value

    other = (1 - core) * 64
    for half, (start, me) in enumerate(((other, z), (other + 32, x))):
        for k, d in enumerate((0, 1, 3, 2)):
            landed(blocks(start + (me + d) % SIDE * 8, 8), 24 + 4 * half + k)
    near_copies = [
        pltpu.make_async_copy(rows(n * RB, RB), table.at[pl.ds(n * RB, RB)], local_sem.at[3 + k])
        for k, n in enumerate((y, up, down))
    ]
    near_copies.append(pltpu.make_async_copy(halo, table.at[pl.ds(SIDE * RB, 128)], local_sem.at[6]))
    for copy in near_copies:
        copy.start()

    @pl.loop(0, RB // 2)
    def _(step):
        for k in range(2):
            r = step * 2 + k
            value = sum_tiles(unpack, plan, r, NEAR, HALO, words, halo, 128)
            totals[pl.ds(pl.multiple_of(r * BLOCK, BLOCK), BLOCK), :] += value

    for copy in near_copies:
        copy.wait()
    landed(far_rows(far * RB), 5)
    landed(far_rows(far * RB + part_half), 6)
    for copy in started:
        copy.wait_send()


def gather(cols, counts, exported, degree, xcur, cached, words):
    hbm = pl.BlockSpec(memory_space=pl.ANY)
    vmem = pl.BlockSpec(memory_space=pltpu.VMEM)
    smem = pl.BlockSpec(memory_space=pltpu.SMEM)
    operands = [
        pltpu.with_memory_space_constraint(a, pltpu.HBM) for a in (cols, counts, degree, xcur, cached, words)
    ]
    operands.insert(2, exported)
    return pl.pallas_call(
        gather_kernel,
        out_shape=(
            pltpu.SMEM((RB, BLOCK), jnp.int32),
            pltpu.VMEM((RB * SLOTS, 16, BLOCK), jnp.int32),
            pltpu.VMEM((256, BLOCK, BLOCK), jnp.bfloat16),
            pltpu.VMEM((ROWS, BLOCK), jnp.float32),
            pltpu.VMEM((ROWS, BLOCK), jnp.float32),
        ),
        in_specs=[hbm, hbm, smem, hbm, hbm, hbm, hbm],
        out_specs=(smem, vmem, vmem, vmem, vmem),
        scratch_shapes=[
            pltpu.VMEM((RB, SLOTS), jnp.int32),
            pltpu.SMEM((RB,), jnp.int32),
            pltpu.VMEM((SIDE, 8, BLOCK), jnp.int32),
            pltpu.VMEM((RB, BLOCK), jnp.int32),
            pltpu.VMEM((RB, BLOCK), jnp.int32),
            pltpu.VMEM((RB, BLOCK, BLOCK), jnp.bfloat16),
            pltpu.VMEM((RB * WORDS, BLOCK), jnp.int32),
            pltpu.VMEM((SIDE * RB, BLOCK, BLOCK), jnp.bfloat16),
            pltpu.VMEM((128, BLOCK, BLOCK), jnp.bfloat16),
            pltpu.SemaphoreType.DMA((11,)),
            pltpu.SemaphoreType.DMA((32,)),
            pltpu.SemaphoreType.DMA((32,)),
        ],
        compiler_params=pltpu.CompilerParams(
            collective_id=0, has_side_effects=True, vmem_limit_bytes=26 * 2**20
        ),
        name="gather",
    )(*operands)


def layer_kernel(
    plan, words, table, before, divisor, w_self, w_neigh, bias, out_hbm, groups, totals, out, turned, out_sem
):
    def out_copy(c):
        span = pl.ds(pl.multiple_of(c * CHUNK * BLOCK, BLOCK), CHUNK * BLOCK)
        return pltpu.make_async_copy(out.at[span], out_hbm.at[span], out_sem.at[c])

    def list_groups(r, at):
        def one(q, at):
            groups[at] = r * 16 + q
            return at + 1

        return lax.fori_loop(0, (plan[r, LEFT] + 3) // 4, one, at)

    total = lax.fori_loop(0, RB, list_groups, 0)
    for k in range(FAN):
        groups[total + k] = -1
    totals[...] = before[...]
    unpack = Unpack()

    def product(at):
        code = groups[at]
        live = code >= 0
        code = jnp.maximum(code, 0)
        r = code >> 4
        first = jnp.where(live, REST + (code & 15) * 4, BLOCK - 8)
        return r, sum_tiles(unpack, plan, r, first, 4, words, table, 256)

    @pl.loop(0, (total + FAN - 1) // FAN)
    def _(step):
        for r, value in [product(step * FAN + k) for k in range(FAN)]:
            totals[pl.ds(pl.multiple_of(r * BLOCK, BLOCK), BLOCK), :] += value

    mine = plan[0, WHO] * RB

    @pl.loop(0, CHUNKS)
    def _(c):
        spans = [pl.ds(pl.multiple_of((c * CHUNK + k) * BLOCK, BLOCK), BLOCK) for k in range(CHUNK)]
        for k in range(CHUNK):
            for m in range(8):
                turned[k, pl.ds(m, 16, stride=8), :] = totals[pl.ds((c * CHUNK + k) * BLOCK + m * 16, 16), :]
        both = []
        for k, span in enumerate(spans):
            average = (turned[k] / divisor[span, :]).astype(jnp.bfloat16)
            own = table[mine + c * CHUNK + k]
            both.append(jnp.concatenate([own, average], axis=1))
        weights = jnp.concatenate([w_self[...], w_neigh[...]], axis=0)
        for span, lhs in zip(spans, both):
            hidden = jnp.dot(lhs, weights, preferred_element_type=jnp.float32) + bias[...]
            out[span, :] = jnp.maximum(hidden, 0.0).astype(jnp.bfloat16)
        out_copy(c).start()

    for c in range(CHUNKS):
        out_copy(c).wait()


def layer(plan, words, table, before, divisor, w_self, w_neigh, bias):
    vmem = pl.BlockSpec(memory_space=pltpu.VMEM)
    smem = pl.BlockSpec(memory_space=pltpu.SMEM)
    hbm = pl.BlockSpec(memory_space=pl.ANY)
    plan = pltpu.with_memory_space_constraint(plan, pltpu.SMEM)
    words, table, before, divisor = (
        pltpu.with_memory_space_constraint(a, pltpu.VMEM) for a in (words, table, before, divisor)
    )
    return pl.pallas_call(
        layer_kernel,
        out_shape=jax.ShapeDtypeStruct((ROWS, 512), jnp.bfloat16),
        in_specs=[smem] + [vmem] * 7,
        out_specs=hbm,
        scratch_shapes=[
            pltpu.SMEM((RB * 10 + FAN,), jnp.int32),
            pltpu.VMEM((ROWS, BLOCK), jnp.float32),
            pltpu.VMEM((ROWS, 512), jnp.bfloat16),
            pltpu.VMEM((CHUNK, BLOCK, BLOCK), jnp.float32),
            pltpu.SemaphoreType.DMA((CHUNKS,)),
        ],
        compiler_params=pltpu.CompilerParams(vmem_limit_bytes=20 * 2**20),
        name="layer",
    )(plan, words, table, before, divisor, w_self, w_neigh, bias.reshape(1, 512))


def on_device(
    x_current, x_cached, w_self, w_neigh, bias, tile_columns, tile_count, adjacency, degree, boundary_blocks
):
    words = adjacency.reshape(RB, 5, 8, 16, BLOCK).transpose(0, 1, 3, 2, 4).reshape(RB * WORDS, BLOCK)
    gathered = gather(
        tile_columns, tile_count, boundary_blocks, degree.reshape(SIDE, 8, BLOCK), x_current.reshape(RB, BLOCK, BLOCK), x_cached.reshape(RB, BLOCK, BLOCK), words
    )
    return layer(*gathered, w_self, w_neigh, bias)


def solution(mesh):
    rows = P(("dom", "grp"), None)
    line = P(("dom", "grp"))
    return jax.shard_map(
        on_device,
        mesh=mesh,
        in_specs=(rows, rows, P(), P(), P(), rows, line, P(("dom", "grp"), None, None), line, rows),
        out_specs=rows,
        check_vma=False,
    )
```

time: 74.7 us -> 58.3 us (0.78)
  Pallas kernels: 70 us -> 56.9 us
  other arithmetic: 3.09 us -> 0 us
    pallas_call x1, Pallas kernels: 25.5 us -> 8.44 us  [layer(): pl.pallas_call(layer_kernel, out_shape=jax.ShapeDtypeStruct((ROWS, 512),...]
    pallas_call x1, Pallas kernels: 44.5 us -> 48.5 us  [gather(): pl.pallas_call(gather_kernel, out_shape=(pltpu.SMEM((RB, BLOCK), jnp.int3...]
    concatenate x1 -> x0, other arithmetic: 1.71 us -> none  [layer(): jnp.concatenate([w_self, w_neigh], axis=0)]
    select_n x1 -> x0, other arithmetic: 1.39 us -> none  [table_index(): return jnp.where(columns < 128, columns, 128 + place)]
where the time goes in v2:
time: 58.3 us; the launch traced here: 57.7 us
  Pallas kernels  56.9 us (98%)
  between operations  0.73 us (1%)
    pallas_call x1, Pallas kernels, gather(): pl.pallas_call(gather_kernel, out_shape=(pltpu.SMEM((RB, BLOCK), jnp.int3...  48.5 us
    pallas_call x1, Pallas kernels, layer(): pl.pallas_call(layer_kernel, out_shape=jax.ShapeDtypeStruct((ROWS, 512),...  8.44 us

profile of v2, /device:TPU:0, one launch (start us, length us, event | category | flops | bytes accessed | tf_op | source)
XLA Modules:
  0.0 57.7 jit_solution(7810848831079987990)
XLA Ops:
  0.0 0.0 copy-start.2
  0.0 0.0 copy-start.1
  0.0 0.0 copy-start
  0.7 48.5 %gather.1 = (s32[32,128]{1,0:T(8,128)S(4)}, s32[1280,16,128]{2,1,0:T(8,128)S(1)}, bf16[256,128,128]{2,1,0:T(8,128)(2,1)S(1)}, f32[4096,128]{1,0:T(8,128)S(1)}, f32[4096,128]{1,0:T(8,128)S(1)}) custom-call(s32[32,40]{1,0:T(8,128)} %cols_hbm.1, s32[32]{0:T(128)} %counts_hbm.1, s32[1,1]{1,0:T(1,128)S(6)} %copy.11.exported, s32[4,8,128]{2,1,0:T(8,128)} %bitcast.13, ...), custom_call_target="tpu_custom_call" | custom-call | tf_op jit(solution)/shard_map/gather/pallas_call | solution.py:287
  49.2 0.0 copy-done.2
  49.2 0.0 copy-done.1
  49.2 0.0 copy-done
  49.2 8.4 %layer.1 = bf16[4096,512]{1,0:T(8,128)(2,1)} custom-call(s32[32,128]{1,0:T(8,128)S(4)} %get-tuple-element.10.plan, s32[1280,16,128]{2,1,0:T(8,128)S(1)} %get-tuple-element.11.words, bf16[256,128,128]{2,1,0:T(8,128)(2,1)S(1)} %get-tuple-element.12.table, f32[4096,128]{1,0:T(8,128)S(1)} %get-tuple-element.13.before, ...), custom_call_target="tpu_custom_call" | custom-call | tf_op jit(solution)/shard_map/layer/pallas_call | solution.py:383
Async XLA Ops:
  0.0 49.2 %copy-start.2 = (f32[512]{0:T(512)S(1)}, f32[512]{0:T(512)}, u32[]{:S(2)}) copy-start(f32[512]{0:T(512)} %param.14) | copy-start | bytes 6148
  0.0 49.2 %copy-start.1 = (bf16[128,512]{1,0:T(8,128)(2,1)S(1)}, bf16[128,512]{1,0:T(8,128)(2,1)}, u32[]{:S(2)}) copy-start(bf16[128,512]{1,0:T(8,128)(2,1)} %w_neigh.1) | copy-start | bytes 393220
  0.0 49.2 %copy-start = (bf16[128,512]{1,0:T(8,128)(2,1)S(1)}, bf16[128,512]{1,0:T(8,128)(2,1)}, u32[]{:S(2)}) copy-start(bf16[128,512]{1,0:T(8,128)(2,1)} %w_self.1) | copy-start | bytes 393220

commit v3 on v2

--- a/solution.py
+++ b/solution.py
@@ -12,11 +12,12 @@
 SLOTS = 40
 WORDS = 640
 ROWS = RB * BLOCK
-NEAR = 12
+SOON = 8
+NEXT = 4
 HALO = 20
 REST = 64
 WHO, LEFT = 126, 127
-FAN = 8
+FAN = 16
 CHUNK = 4
 CHUNKS = RB // CHUNK
 
@@ -29,25 +30,31 @@
     c = wide[...]
     t = lax.broadcasted_iota(jnp.int32, (RB, BLOCK), 1)
     on = t < live[...]
-    far = (((c >> 5) - me) & 3) == 2
-    kind = jnp.where(on, jnp.where(c < 128, jnp.where(far, 2, 0), 1), 3)
+    d, b = ((c >> 5) - me) & 3, c & 31
+    soon = (d == 0) | ((d == 3) & (b < 16)) | ((d == 1) & (b >= 16))
     e = c - 128
     y, core, z, x = e & 3, (e >> 2) & 1, (e >> 3) & 3, (e >> 5) & 3
     place = core * 64 + (y >> 1) * 32 + jnp.where(y < 2, z * 4 + x, x * 4 + z) * 2 + (y & 1)
-    index = jnp.where(c < 128, c, 128 + place)
-    entry = t | (index << 10) | (1 << 18)
-    both = (kind << 19) | entry
+    inside = c < 128
+    kind = jnp.where(inside, jnp.where(soon, 0, jnp.where(d == 2, 3, 1)), 2)
+    both = jnp.where(on, kind, 4) << 22
+    near_place = jnp.where(d == 0, b, jnp.where(soon, 32 + b, jnp.where(d == 3, b & 15, 16 + (b & 15))))
+    index = (jnp.where(inside, near_place, place) << 6) | (jnp.where(inside, c, 128 + place) << 13)
+    both = both | t | index | (1 << 21)
     table = jnp.zeros((RB, BLOCK), jnp.int32)
-    nears = halos = rests = jnp.zeros((RB, BLOCK), jnp.int32)
+    soons = nexts = halos = rests = jnp.zeros((RB, BLOCK), jnp.int32)
     for s in range(SLOTS):
         one = jnp.broadcast_to(both[:, s : s + 1], (RB, BLOCK))
-        kind = one >> 19
-        near = (kind == 0) & (nears < NEAR)
-        halo = (kind == 1) & (halos < HALO)
-        rest = (kind < 3) & jnp.logical_not(near | halo)
-        target = jnp.where(near, nears, jnp.where(halo, NEAR + halos, jnp.where(rest, REST + rests, -1)))
-        table = jnp.where(target == t, one & ((1 << 19) - 1), table)
-        nears += jnp.where(near, 1, 0)
+        kind = one >> 22
+        soon = (kind == 0) & (soons < SOON)
+        after = (kind == 1) & (nexts < NEXT)
+        halo = (kind == 2) & (halos < HALO)
+        rest = (kind < 4) & jnp.logical_not(soon | after | halo)
+        target = jnp.where(halo, SOON + NEXT + halos, jnp.where(rest, REST + rests, -1))
+        target = jnp.where(soon, soons, jnp.where(after, SOON + nexts, target))
+        table = jnp.where(target == t, one & ((1 << 22) - 1), table)
+        soons += jnp.where(soon, 1, 0)
+        nexts += jnp.where(after, 1, 0)
         halos += jnp.where(halo, 1, 0)
         rests += jnp.where(rest, 1, 0)
     table = jnp.where(t == LEFT, rests, jnp.where(t == WHO, me, table))
@@ -80,14 +87,14 @@
         return [jnp.concatenate(tile, axis=0) for tile in tiles]
 
 
-def sum_tiles(unpack, plan, r, first, count, words, table, blocks):
+def sum_tiles(unpack, plan, r, first, count, words, table, shift, blocks):
     tiles, features = [], []
     for group in range(count // 4):
         entries = [plan[r, first + group * 4 + k] for k in range(4)]
-        rows = [r * SLOTS + (e & 1023) for e in entries]
-        tiles += unpack.four(words, rows, [-(e >> 18) for e in entries])
+        rows = [r * SLOTS + (e & 63) for e in entries]
+        tiles += unpack.four(words, rows, [-(e >> 21) for e in entries])
         for e in entries:
-            block = (e >> 10) & (blocks - 1)
+            block = (e >> shift) & (blocks - 1)
             features.append(table[block])
     return jnp.dot(
         jnp.concatenate(tiles, axis=1), jnp.concatenate(features, axis=0), preferred_element_type=jnp.float32
@@ -97,7 +104,7 @@
 def gather_kernel(
     cols_hbm, counts_hbm, exported, degree_hbm, xcur, cached_hbm, words_hbm,
     plan, words, table, totals, divisor,
-    cols, counts, degree, wide, live, cached, raw, part, halo, local_sem, send_sem, recv_sem,
+    cols, counts, degree, wide, live, cached, raw, soon, after, halo, local_sem, send_sem, recv_sem,
 ):
     dom = lax.axis_index("dom")
     y = lax.axis_index("grp")
@@ -158,8 +165,9 @@
     def blocks(first, count):
         return halo.at[pl.ds(first, count)]
 
-    def rows(first, count):
-        return part.at[pl.ds(first, count)]
+    part_half = RB // 2
+    halves = pl.ds(0, part_half), pl.ds(part_half, part_half)
+    from_down, from_up = soon.at[pl.ds(RB, part_half)], soon.at[pl.ds(RB + part_half, part_half)]
 
     def far_rows(first):
         return table.at[pl.ds(first, RB // 2)]
@@ -171,7 +179,6 @@
         return base + (yy // 2) * 32 + ring * 2 + yy % 2
 
     own = blocks(place(y), 1)
-    own_part = rows(y * RB, RB)
     cached_copy.wait()
     for copy in small_copies:
         copy.wait()
@@ -179,9 +186,9 @@
     halo[place(y)] = chosen
     for sem, peer in enumerate((y_up, y_down, y_far)):
         send(own, own, sem, peer)
-    send(xcur, own_part, 3, y_up)
-    send(xcur, own_part, 4, y_down)
-    part_copy = pltpu.make_async_copy(xcur, own_part, local_sem.at[1])
+    send(xcur.at[halves[0]], from_down, 3, y_up)
+    send(xcur.at[halves[1]], from_up, 4, y_down)
+    part_copy = pltpu.make_async_copy(xcur, soon.at[pl.ds(0, RB)], local_sem.at[1])
     part_copy.start()
     wide[...] = sort_slots(cols, counts, y, wide, live)
     plan_copy = pltpu.make_async_copy(wide, plan, local_sem.at[0])
@@ -210,6 +217,9 @@
             slot = raw[pl.ds(r * WORDS + (t // 8) * BLOCK + t % 8, 16, stride=8), :]
             words[r * SLOTS + t] = slot
 
+    send(xcur.at[halves[1]], after.at[halves[0]], 32, y_up)
+    send(xcur.at[halves[0]], after.at[halves[1]], 33, y_down)
+
     for half, (piece, me, _) in enumerate(first):
         for k, d in enumerate((1, 3, 2)):
             landed(blocks(piece((me + d) % SIDE), 2), 8 + 4 * half + k)
@@ -230,45 +240,51 @@
             landed(got, 16 + 4 * half + k)
             send(got, got, 25 + 4 * half + k, sibling)
 
+    part_copy.wait()
+    plan_copy.wait()
+    landed(from_down, 3)
+    landed(from_up, 4)
+    unpack = Unpack()
+
+    def add_tiles(first, count, source, each, start=False):
+        @pl.loop(0, RB // each)
+        def _(step):
+            for k in range(each):
+                r = step * each + k
+                value = sum_tiles(unpack, plan, r, first, count, words, source, 6, source.shape[0])
+                span = pl.ds(pl.multiple_of(r * BLOCK, BLOCK), BLOCK)
+                totals[span, :] = value if start else totals[span, :] + value
+
+    send(from_down, far_rows(down * RB), 5, y_up)
+    send(from_up, far_rows(up * RB + part_half), 6, y_down)
+    add_tiles(0, SOON, soon, 8, start=True)
+
+    def keep(k, src, first):
+        copy = pltpu.make_async_copy(src, table.at[pl.ds(first, src.shape[0])], local_sem.at[k])
+        copy.start()
+        return copy
+
     pass_on(0, 1)
     pass_on(1, 3)
-    part_half = RB // 2
-    landed(rows(down * RB, RB), 3)
-    send(rows(down * RB, part_half), far_rows(down * RB), 5, y_up)
-    landed(rows(up * RB, RB), 4)
-    send(rows(up * RB + part_half, part_half), far_rows(up * RB + part_half), 6, y_down)
     pass_on(2, 2)
-    part_copy.wait()
-    plan_copy.wait()
-    unpack = Unpack()
-
-    @pl.loop(0, RB // 4)
-    def _(step):
-        for k in range(4):
-            r = step * 4 + k
-            value = sum_tiles(unpack, plan, r, 0, NEAR, words, part, 128)
-            totals[pl.ds(pl.multiple_of(r * BLOCK, BLOCK), BLOCK), :] = value
+    landed(after.at[halves[0]], 32)
+    landed(after.at[halves[1]], 33)
+    kept = [
+        keep(3, soon.at[pl.ds(0, RB)], y * RB),
+        keep(4, from_down, down * RB),
+        keep(5, from_up, up * RB + part_half),
+        keep(6, after.at[halves[0]], down * RB + part_half),
+        keep(0, after.at[halves[1]], up * RB),
+    ]
+    add_tiles(SOON, NEXT, after, 8)
 
     other = (1 - core) * 64
     for half, (start, me) in enumerate(((other, z), (other + 32, x))):
         for k, d in enumerate((0, 1, 3, 2)):
             landed(blocks(start + (me + d) % SIDE * 8, 8), 24 + 4 * half + k)
-    near_copies = [
-        pltpu.make_async_copy(rows(n * RB, RB), table.at[pl.ds(n * RB, RB)], local_sem.at[3 + k])
-        for k, n in enumerate((y, up, down))
-    ]
-    near_copies.append(pltpu.make_async_copy(halo, table.at[pl.ds(SIDE * RB, 128)], local_sem.at[6]))
-    for copy in near_copies:
-        copy.start()
-
-    @pl.loop(0, RB // 2)
-    def _(step):
-        for k in range(2):
-            r = step * 2 + k
-            value = sum_tiles(unpack, plan, r, NEAR, HALO, words, halo, 128)
-            totals[pl.ds(pl.multiple_of(r * BLOCK, BLOCK), BLOCK), :] += value
-
-    for copy in near_copies:
+    kept.append(keep(1, halo, SIDE * RB))
+    add_tiles(SOON + NEXT, HALO, halo, 4)
+    for copy in kept:
         copy.wait()
     landed(far_rows(far * RB), 5)
     landed(far_rows(far * RB + part_half), 6)
@@ -303,11 +319,12 @@
             pltpu.VMEM((RB, BLOCK), jnp.int32),
             pltpu.VMEM((RB, BLOCK, BLOCK), jnp.bfloat16),
             pltpu.VMEM((RB * WORDS, BLOCK), jnp.int32),
-            pltpu.VMEM((SIDE * RB, BLOCK, BLOCK), jnp.bfloat16),
+            pltpu.VMEM((2 * RB, BLOCK, BLOCK), jnp.bfloat16),
+            pltpu.VMEM((RB, BLOCK, BLOCK), jnp.bfloat16),
             pltpu.VMEM((128, BLOCK, BLOCK), jnp.bfloat16),
             pltpu.SemaphoreType.DMA((11,)),
-            pltpu.SemaphoreType.DMA((32,)),
-            pltpu.SemaphoreType.DMA((32,)),
+            pltpu.SemaphoreType.DMA((34,)),
+            pltpu.SemaphoreType.DMA((34,)),
         ],
         compiler_params=pltpu.CompilerParams(
             collective_id=0, has_side_effects=True, vmem_limit_bytes=26 * 2**20
@@ -342,7 +359,7 @@
         code = jnp.maximum(code, 0)
         r = code >> 4
         first = jnp.where(live, REST + (code & 15) * 4, BLOCK - 8)
-        return r, sum_tiles(unpack, plan, r, first, 4, words, table, 256)
+        return r, sum_tiles(unpack, plan, r, first, 4, words, table, 13, 256)
 
     @pl.loop(0, (total + FAN - 1) // FAN)
     def _(step):

time: 58.3 us -> 53.4 us (0.916)
  the two profiles are of different devices: /device:TPU:0 before, /device:TPU:1 now
where the time goes in v3:
time: 53.4 us; the launch traced here: 53 us
  Pallas kernels  52.3 us (98%)
  between operations  0.73 us (1%)
    pallas_call x1, Pallas kernels, gather(): pl.pallas_call(gather_kernel, out_shape=(pltpu.SMEM((RB, BLOCK), jnp.int3...  44.2 us
    pallas_call x1, Pallas kernels, layer(): pl.pallas_call(layer_kernel, out_shape=jax.ShapeDtypeStruct((ROWS, 512),...  8.07 us

profile of v3, /device:TPU:1, one launch (start us, length us, event | category | flops | bytes accessed | tf_op | source)
XLA Modules:
  0.0 53.0 jit_solution(17507290398905019616)
XLA Ops:
  0.0 0.0 copy-start.2
  0.0 0.0 copy-start.1
  0.0 0.0 copy-start
  0.7 44.2 %gather.1 = (s32[32,128]{1,0:T(8,128)S(4)}, s32[1280,16,128]{2,1,0:T(8,128)S(1)}, bf16[256,128,128]{2,1,0:T(8,128)(2,1)S(1)}, f32[4096,128]{1,0:T(8,128)S(1)}, f32[4096,128]{1,0:T(8,128)S(1)}) custom-call(s32[32,40]{1,0:T(8,128)} %cols_hbm.1, s32[32]{0:T(128)} %counts_hbm.1, s32[1,1]{1,0:T(1,128)S(6)} %copy.11.exported, s32[4,8,128]{2,1,0:T(8,128)} %bitcast.13, ...), custom_call_target="tpu_custom_call" | custom-call | tf_op jit(solution)/shard_map/gather/pallas_call | solution.py:303
  45.0 0.0 copy-done.2
  45.0 0.0 copy-done.1
  45.0 0.0 copy-done
  45.0 8.1 %layer.1 = bf16[4096,512]{1,0:T(8,128)(2,1)} custom-call(s32[32,128]{1,0:T(8,128)S(4)} %get-tuple-element.10.plan, s32[1280,16,128]{2,1,0:T(8,128)S(1)} %get-tuple-element.11.words, bf16[256,128,128]{2,1,0:T(8,128)(2,1)S(1)} %get-tuple-element.12.table, f32[4096,128]{1,0:T(8,128)S(1)} %get-tuple-element.13.before, ...), custom_call_target="tpu_custom_call" | custom-call | tf_op jit(solution)/shard_map/layer/pallas_call | solution.py:400
Async XLA Ops:
  0.0 45.0 %copy-start.2 = (f32[512]{0:T(512)S(1)}, f32[512]{0:T(512)}, u32[]{:S(2)}) copy-start(f32[512]{0:T(512)} %param.14) | copy-start | bytes 6148
  0.0 45.0 %copy-start.1 = (bf16[128,512]{1,0:T(8,128)(2,1)S(1)}, bf16[128,512]{1,0:T(8,128)(2,1)}, u32[]{:S(2)}) copy-start(bf16[128,512]{1,0:T(8,128)(2,1)} %w_neigh.1) | copy-start | bytes 393220
  0.0 45.0 %copy-start = (bf16[128,512]{1,0:T(8,128)(2,1)S(1)}, bf16[128,512]{1,0:T(8,128)(2,1)}, u32[]{:S(2)}) copy-start(bf16[128,512]{1,0:T(8,128)(2,1)} %w_self.1) | copy-start | bytes 393220

commit v4 on v3

--- a/solution.py
+++ b/solution.py
@@ -18,7 +18,7 @@
 REST = 64
 WHO, LEFT = 126, 127
 FAN = 16
-CHUNK = 4
+CHUNK = 8
 CHUNKS = RB // CHUNK
 
 

time: 53.4 us -> 52.3 us (0.979)
  the two profiles are of different devices: /device:TPU:1 before, /device:TPU:0 now
where the time goes in v4:
time: 52.3 us; the launch traced here: 52.2 us
  Pallas kernels  51.4 us (98%)
  between operations  0.73 us (1%)
    pallas_call x1, Pallas kernels, gather(): pl.pallas_call(gather_kernel, out_shape=(pltpu.SMEM((RB, BLOCK), jnp.int3...  44 us
    pallas_call x1, Pallas kernels, layer(): pl.pallas_call(layer_kernel, out_shape=jax.ShapeDtypeStruct((ROWS, 512),...  7.45 us

profile of v4, /device:TPU:0, one launch (start us, length us, event | category | flops | bytes accessed | tf_op | source)
XLA Modules:
  0.0 52.2 jit_solution(5480499500779518915)
XLA Ops:
  0.0 0.0 copy-start.2
  0.0 0.0 copy-start.1
  0.0 0.0 copy-start
  0.7 44.0 %gather.1 = (s32[32,128]{1,0:T(8,128)S(4)}, s32[1280,16,128]{2,1,0:T(8,128)S(1)}, bf16[256,128,128]{2,1,0:T(8,128)(2,1)S(1)}, f32[4096,128]{1,0:T(8,128)S(1)}, f32[4096,128]{1,0:T(8,128)S(1)}) custom-call(s32[32,40]{1,0:T(8,128)} %cols_hbm.1, s32[32]{0:T(128)} %counts_hbm.1, s32[1,1]{1,0:T(1,128)S(6)} %copy.11.exported, s32[4,8,128]{2,1,0:T(8,128)} %bitcast.13, ...), custom_call_target="tpu_custom_call" | custom-call | tf_op jit(solution)/shard_map/gather/pallas_call | solution.py:303
  44.7 0.0 copy-done.2
  44.7 0.0 copy-done.1
  44.7 0.0 copy-done
  44.7 7.5 %layer.1 = bf16[4096,512]{1,0:T(8,128)(2,1)} custom-call(s32[32,128]{1,0:T(8,128)S(4)} %get-tuple-element.10.plan, s32[1280,16,128]{2,1,0:T(8,128)S(1)} %get-tuple-element.11.words, bf16[256,128,128]{2,1,0:T(8,128)(2,1)S(1)} %get-tuple-element.12.table, f32[4096,128]{1,0:T(8,128)S(1)} %get-tuple-element.13.before, ...), custom_call_target="tpu_custom_call" | custom-call | tf_op jit(solution)/shard_map/layer/pallas_call | solution.py:400
Async XLA Ops:
  0.0 44.7 %copy-start.2 = (f32[512]{0:T(512)S(1)}, f32[512]{0:T(512)}, u32[]{:S(2)}) copy-start(f32[512]{0:T(512)} %param.14) | copy-start | bytes 6148
  0.0 44.7 %copy-start.1 = (bf16[128,512]{1,0:T(8,128)(2,1)S(1)}, bf16[128,512]{1,0:T(8,128)(2,1)}, u32[]{:S(2)}) copy-start(bf16[128,512]{1,0:T(8,128)(2,1)} %w_neigh.1) | copy-start | bytes 393220
  0.0 44.7 %copy-start = (bf16[128,512]{1,0:T(8,128)(2,1)S(1)}, bf16[128,512]{1,0:T(8,128)(2,1)}, u32[]{:S(2)}) copy-start(bf16[128,512]{1,0:T(8,128)(2,1)} %w_self.1) | copy-start | bytes 393220
